TPU v7x, 32 devices: a whole 2x2x4 slice. The times are simulated.
32 devices in a mesh: dp: 2 (over x), row: 4 (over z), col: 4 (over y, core).
Axes of the slice: x: 2, y: 2, z: 4, core: 2. Of those that a mesh axis runs over, the one named last changes fastest.
Arguments:
- x_in: bfloat16 [16384, 1024], P(('dp', 'col'), 'row'), may hold values from -6 to 6
- ln1_gain: float32 [1024], P('row'), may hold values from 0.5 to 1.5
- ln1_bias: float32 [1024], P('row'), may hold values from -1.5 to 1.5
- w_qkv: bfloat16 [1024, 3072], P('row', 'col'), may hold values from -0.1875 to 0.1875
- bias_qv: float32 [2048], P('col'), may hold values from -1.5 to 1.5
- w_out: bfloat16 [1024, 1024], P('col', 'row'), may hold values from -0.375 to 0.375
- b_out: float32 [1024], P('row'), may hold values from -1.5 to 1.5
- ln2_gain: float32 [1024], P('row'), may hold values from 0.5 to 1.5
- ln2_bias: float32 [1024], P('row'), may hold values from -1.5 to 1.5
- w_up: bfloat16 [1024, 4096], P('row', 'col'), may hold values from -0.1875 to 0.1875
- b_up: float32 [4096], P('col'), may hold values from -1.5 to 1.5
- w_down: bfloat16 [4096, 1024], P('col', 'row'), may hold values from -0.09375 to 0.09375
- b_down: float32 [1024], P('row'), may hold values from -1.5 to 1.5
- grad_out: bfloat16 [16384, 1024], P(('dp', 'col'), 'row'), may hold values from -6 to 6
Outputs:
- out: bfloat16 [16384, 1024], P(('dp', 'col'), 'row')
- grad_input: bfloat16 [16384, 1024], P(('dp', 'col'), 'row')
- grad_ln1_gain: float32 [1024], P('row')
- grad_ln1_bias: float32 [1024], P('row')
- grad_qkv: float32 [1024, 3072], P('row', 'col')
- grad_bias_qv: float32 [2048], P('col')
- grad_w_out: float32 [1024, 1024], P('col', 'row')
- grad_b_out: float32 [1024], P('row')
- grad_ln2_gain: float32 [1024], P('row')
- grad_ln2_bias: float32 [1024], P('row')
- grad_up: float32 [1024, 4096], P('row', 'col')
- grad_b_up: float32 [4096], P('col')
- grad_down: float32 [4096, 1024], P('col', 'row')
- grad_b_down: float32 [1024], P('row')
All inputs are finite; a program needn't handle non-finite values.
Results may differ from a plain program's by a relative error of at most 0.0098.
Values may be sent and summed in bfloat16 or wider, within the bound.
A program may use at most 192 MiB of HBM per device.

v0:
```python
import jax
import jax.numpy as jnp
from jax import lax
from jax.sharding import PartitionSpec as P

D = 1024
HEADS = 16
HEAD = 64
LEN = 1024


EPSILON = 1e-05


def gelu(value):
    return (
        0.5
        * value
        * (1.0 + jnp.tanh(0.7978845608028654 * (value + 0.044715 * value * value * value)))
    )


def contract_rows(left, right):
    return lax.dot_general(
        left, right, (((0,), (0,)), ((), ())), preferred_element_type=jnp.float32
    )


def row_totals(first, second):
    return lax.psum((first, second), "row")


def gather_cols(value):
    return lax.all_gather(value, "col", axis=0, tiled=True)


def sum_cols(whole, weight, flipped):
    axis_right = 1 if flipped else 0
    return lax.psum_scatter(
        lax.dot_general(
            whole, weight, (((1,), (axis_right,)), ((), ())), preferred_element_type=jnp.float32
        ),
        "col",
        scatter_dimension=0,
        tiled=True,
    )


def hidden_share(whole, weight, flipped):
    axis_right = 1 if flipped else 0
    return lax.psum_scatter(
        lax.dot_general(
            whole, weight, (((1,), (axis_right,)), ((), ())), preferred_element_type=jnp.float32
        ),
        "row",
        scatter_dimension=0,
        tiled=True,
    )


def hidden_rows(value):
    return lax.all_gather(value, "row", axis=0, tiled=True)


def norm_forward(values, gain, shift):
    total, square = row_totals(jnp.sum(values, 1), jnp.sum(values * values, 1))
    center = total / D
    spread = square / D - center * center
    inverse = lax.rsqrt(spread + EPSILON)
    scaled = (values - center[:, None]) * inverse[:, None]
    return ((scaled * gain + shift).astype(jnp.bfloat16), scaled, inverse)


def norm_backward(grad_normed, scaled, inverse, gain):
    product = grad_normed * gain
    first, second = row_totals(jnp.sum(product, 1), jnp.sum(product * scaled, 1))
    grad_values = inverse[:, None] * (product - first[:, None] / D - scaled * second[:, None] / D)
    return (grad_values, jnp.sum(grad_normed * scaled, 0), jnp.sum(grad_normed, 0))


def on_device(
    x_in,
    ln1_gain,
    ln1_bias,
    w_qkv,
    bias_qv,
    w_out,
    b_out,
    ln2_gain,
    ln2_bias,
    w_up,
    b_up,
    w_down,
    b_down,
    grad_out,
):
    row_count = x_in.shape[0]
    seq_count = row_count // LEN
    local_heads = w_qkv.shape[1] // (3 * HEAD)
    block = min(512, LEN)
    block_count = LEN // block
    head_ids = lax.axis_index("col") * local_heads + jnp.arange(local_heads)
    slopes = 2.0 ** (-8.0 * (head_ids.astype(jnp.float32) + 1.0) / HEADS)
    key_place = jnp.arange(LEN)

    def scores_of(query_block, keys, index):
        raw = (
            jnp.einsum("qhe,khe->hqk", query_block, keys, preferred_element_type=jnp.float32)
            * 0.125
        )
        query_place = index * block + jnp.arange(block)
        distance = (query_place[:, None] - key_place[None, :]).astype(jnp.float32)
        scores = raw - slopes[:, None, None] * distance[None]
        return jnp.where(distance[None] >= 0, scores, -jnp.inf)

    inputs = x_in.astype(jnp.float32)
    normed_one, scaled_one, inverse_one = norm_forward(inputs, ln1_gain, ln1_bias)
    gathered_one = gather_cols(normed_one)
    piece = gathered_one
    joined = lax.psum_scatter(
        jnp.dot(piece, w_qkv, preferred_element_type=jnp.float32),
        "row",
        scatter_dimension=0,
        tiled=True,
    )
    pair = bias_qv.reshape(local_heads, 2, HEAD)
    full_bias = jnp.stack([pair[:, 0], jnp.zeros_like(pair[:, 0]), pair[:, 1]], 1).reshape(-1)
    joined_low = (
        (joined + full_bias).astype(jnp.bfloat16).reshape(seq_count, LEN, local_heads, 3, HEAD)
    )
    query = joined_low[:, :, :, 0]
    keys = joined_low[:, :, :, 1]
    values = joined_low[:, :, :, 2]

    def attend_sequence(triple):
        seq_query, seq_keys, seq_values = triple

        def attend_block(index):
            query_block = lax.dynamic_slice_in_dim(seq_query, index * block, block, 0)
            scores = scores_of(query_block, seq_keys, index)
            top = jnp.max(scores, -1)
            expo = jnp.exp(scores - top[..., None])
            total = jnp.sum(expo, -1)
            probs = (expo / total[..., None]).astype(jnp.bfloat16)
            result = jnp.einsum(
                "hqk,khe->qhe", probs, seq_values, preferred_element_type=jnp.float32
            )
            return (result.astype(jnp.bfloat16), top + jnp.log(total))

        return lax.map(attend_block, jnp.arange(block_count))

    context_blocks, log_totals = lax.map(attend_sequence, (query, keys, values))
    context = context_blocks.reshape(row_count, local_heads * HEAD)
    context_all = lax.all_gather(context, "row", axis=0, tiled=True)
    middle = inputs + sum_cols(context_all, w_out, False) + b_out
    normed_two, scaled_two, inverse_two = norm_forward(middle, ln2_gain, ln2_bias)
    gathered_two = gather_cols(normed_two)
    hidden = hidden_share(gathered_two, w_up, False) + b_up
    active_all = hidden_rows(gelu(hidden).astype(jnp.bfloat16))
    out = (middle + sum_cols(active_all, w_down, False) + b_down).astype(jnp.bfloat16)
    cotangent = grad_out.astype(jnp.float32)
    grad_b_down = jnp.sum(cotangent, 0)
    cotangent_all = gather_cols(grad_out)
    grad_down = contract_rows(active_all, cotangent_all)
    _, gelu_pull = jax.vjp(gelu, hidden)
    grad_active = hidden_share(cotangent_all, w_down, True)
    grad_hidden_all = hidden_rows(gelu_pull(grad_active)[0].astype(jnp.bfloat16))
    grad_b_up = jnp.sum(grad_hidden_all.astype(jnp.float32), 0)
    grad_up = contract_rows(gathered_two, grad_hidden_all)
    grad_normed_two = sum_cols(grad_hidden_all, w_up, True)
    back_two, grad_ln2_gain, grad_ln2_bias = norm_backward(
        grad_normed_two, scaled_two, inverse_two, ln2_gain
    )
    grad_middle = cotangent + back_two
    grad_b_out = jnp.sum(grad_middle, 0)
    grad_middle_all = gather_cols(grad_middle.astype(jnp.bfloat16))
    grad_w_out = contract_rows(context_all, grad_middle_all)
    piece = grad_middle_all
    grad_context = lax.psum_scatter(
        lax.dot_general(piece, w_out, (((1,), (1,)), ((), ())), preferred_element_type=jnp.float32),
        "row",
        scatter_dimension=0,
        tiled=True,
    ).astype(jnp.bfloat16)
    grad_context = grad_context.reshape(seq_count, LEN, local_heads, HEAD)

    def back_sequence(group):
        seq_query, seq_keys, seq_values, seq_grad, seq_log = group

        def back_block(carry, index):
            grad_keys, grad_values = carry
            query_block = lax.dynamic_slice_in_dim(seq_query, index * block, block, 0)
            grad_block = lax.dynamic_slice_in_dim(seq_grad, index * block, block, 0)
            scores = scores_of(query_block, seq_keys, index)
            probs = jnp.exp(scores - seq_log[index][..., None])
            probs_low = probs.astype(jnp.bfloat16)
            grad_probs = jnp.einsum(
                "qhe,khe->hqk", grad_block, seq_values, preferred_element_type=jnp.float32
            )
            inner = jnp.sum(probs * grad_probs, -1, keepdims=True)
            grad_scores = (probs * (grad_probs - inner)).astype(jnp.bfloat16)
            grad_query = (
                jnp.einsum(
                    "hqk,khe->qhe", grad_scores, seq_keys, preferred_element_type=jnp.float32
                )
                * 0.125
            )
            grad_keys = (
                grad_keys
                + jnp.einsum(
                    "hqk,qhe->khe", grad_scores, query_block, preferred_element_type=jnp.float32
                )
                * 0.125
            )
            grad_values = grad_values + jnp.einsum(
                "hqk,qhe->khe", probs_low, grad_block, preferred_element_type=jnp.float32
            )
            return ((grad_keys, grad_values), grad_query)

        empty = jnp.zeros((LEN, local_heads, HEAD), jnp.float32)
        (grad_keys, grad_values), grad_queries = lax.scan(
            back_block, (empty, empty), jnp.arange(block_count)
        )
        return (grad_queries.reshape(LEN, local_heads, HEAD), grad_keys, grad_values)

    grad_query, grad_keys, grad_values = lax.map(
        back_sequence, (query, keys, values, grad_context, log_totals)
    )
    grad_joined = jnp.stack([grad_query, grad_keys, grad_values], 3).reshape(
        row_count, 3 * local_heads * HEAD
    )
    grad_joined_all = lax.all_gather(grad_joined.astype(jnp.bfloat16), "row", axis=0, tiled=True)
    column_totals = jnp.sum(grad_joined_all.astype(jnp.float32), 0).reshape(local_heads, 3, HEAD)
    grad_bias_qv = jnp.stack([column_totals[:, 0], column_totals[:, 2]], 1).reshape(-1)
    grad_qkv = contract_rows(gathered_one, grad_joined_all)
    grad_normed_one = sum_cols(grad_joined_all, w_qkv, True)
    back_one, grad_ln1_gain, grad_ln1_bias = norm_backward(
        grad_normed_one, scaled_one, inverse_one, ln1_gain
    )
    grad_input = (grad_middle + back_one).astype(jnp.bfloat16)
    grad_qkv, grad_bias_qv, grad_w_out, grad_up, grad_b_up, grad_down = lax.psum(
        (grad_qkv, grad_bias_qv, grad_w_out, grad_up, grad_b_up, grad_down), "dp"
    )
    grad_ln1_gain, grad_ln1_bias, grad_b_out, grad_ln2_gain, grad_ln2_bias, grad_b_down = lax.psum(
        (grad_ln1_gain, grad_ln1_bias, grad_b_out, grad_ln2_gain, grad_ln2_bias, grad_b_down),
        ("dp", "col"),
    )
    return (
        out,
        grad_input,
        grad_ln1_gain,
        grad_ln1_bias,
        grad_qkv,
        grad_bias_qv,
        grad_w_out,
        grad_b_out,
        grad_ln2_gain,
        grad_ln2_bias,
        grad_up,
        grad_b_up,
        grad_down,
        grad_b_down,
    )


def solution(mesh):
    in_specs = (
        P(("dp", "col"), "row"),
        P("row"),
        P("row"),
        P("row", "col"),
        P("col"),
        P("col", "row"),
        P("row"),
        P("row"),
        P("row"),
        P("row", "col"),
        P("col"),
        P("col", "row"),
        P("row"),
        P(("dp", "col"), "row"),
    )
    out_specs = (
        P(("dp", "col"), "row"),
        P(("dp", "col"), "row"),
        P("row"),
        P("row"),
        P("row", "col"),
        P("col"),
        P("col", "row"),
        P("row"),
        P("row"),
        P("row"),
        P("row", "col"),
        P("col"),
        P("col", "row"),
        P("row"),
    )
    return jax.shard_map(
        on_device, mesh=mesh, in_specs=in_specs, out_specs=out_specs, check_vma=False
    )
```

profile of v0, /device:TPU:0, one launch (start us, length us, event | category | flops | bytes accessed | tf_op | source)
XLA Modules:
  0.0 3346.3 jit_solution(9530168090227756145)
XLA Ops:
  9.2 20.5 all-reduce.4
  32.9 32.8 all-gather.9.cloned.1.call-done
  65.7 13.9 fusion.67
  80.7 413.6 %reduce-scatter.9.cloned.1.call-done = f32[2048,768]{1,0:T(8,128)} async-done(((f32[8192,768]{1,0:T(8,128)}), f32[2048,768]{1,0:T(8,128)}) %reduce-scatter.9.cloned.1.call-update) | async-done | bytes 6291472 | tf_op jit(solution)/shard_map/reduce_scatter | solution.py:120
  517.4 52.0 %while.58 = (s32[]{:T(128)}, bf16[2,2,512,4,64]{2,1,0,4,3:T(2,128)(2,1)}, f32[2,2,4,512]{3,2,1,0:T(4,128)S(1)}, bf16[2,1024,4,64]{1,3,2,0:T(8,128)(2,1)}, bf16[2...) while((s32[]{:T(128)}, ...), condition=%wide.region_10.11_spmd.clone, body=%wide.region_5.10_spmd.clone.sunk | while | flops 577370624 | bytes 41537020 | solution.py:152
  519.9 22.2 while.61
  545.8 22.2 while.61
  572.0 82.7 %all-gather.11.cloned.1.call-done = bf16[8192,256]{0,1:T(8,128)(2,1)} async-done(((bf16[2048,256]{0,1:T(8,128)(2,1)}), bf16[8192,256]{0,1:T(8,128)(2,1)}) %all-gather.11.cloned.1.call-update) | async-done | bytes 4194320 | tf_op jit(solution)/shard_map/all_gather | solution.py:154
  662.4 69.5 %reduce-scatter.11.cloned.1.call-done = f32[2048,256]{1,0:T(8,128)} async-done(((f32[8192,256]{1,0:T(8,128)}), f32[2048,256]{1,0:T(8,128)}) %reduce-scatter.11.cloned.1.call-update) | async-done | bytes 2097168 | tf_op jit(solution)/shard_map/reduce_scatter | solution.py:39
  734.4 18.7 all-reduce.3
  767.8 16.6 fusion.71
  784.5 19.8 all-gather.13.cloned.1.call-done
  804.3 15.9 fusion.69
  820.3 538.5 %reduce-scatter.17.cloned.1.call-done = f32[2048,1024]{1,0:T(8,128)} async-done(((f32[8192,1024]{1,0:T(8,128)}), f32[2048,1024]{1,0:T(8,128)}) %reduce-scatter.17.cloned.1.call-update) | async-done | bytes 8388624 | tf_op jit(solution)/shard_map/reduce_scatter | solution.py:51
  1358.7 555.3 %reduce-scatter.13.cloned.1.call-done = f32[2048,1024]{1,0:T(8,128)} async-done(((f32[8192,1024]{1,0:T(8,128)}), f32[2048,1024]{1,0:T(8,128)}) %reduce-scatter.13.cloned.1.call-update) | async-done | bytes 8388624 | tf_op jit(solution)/shard_map/reduce_scatter | solution.py:51
  1928.3 286.6 %all-gather.19.cloned.1.call-done = bf16[8192,1024]{1,0:T(8,128)(2,1)} async-done(((bf16[2048,1024]{1,0:T(8,128)(2,1)}), bf16[8192,1024]{1,0:T(8,128)(2,1)}) %all-gather.19.cloned.1.call-update) | async-done | bytes 16777232 | tf_op jit(solution)/shard_map/all_gather | solution.py:62
  2214.9 14.2 fusion.72
  2229.1 272.2 %all-gather.15.cloned.1.call-done = bf16[8192,1024]{1,0:T(8,128)(2,1)} async-done(((bf16[2048,1024]{1,0:T(8,128)(2,1)}), bf16[8192,1024]{1,0:T(8,128)(2,1)}) %all-gather.15.cloned.1.call-update) | async-done | bytes 16777232 | tf_op jit(solution)/shard_map/all_gather | solution.py:62
  2501.3 15.1 fusion.70
  2516.5 57.4 %reduce-scatter.19.cloned.1.call-done = f32[2048,256]{1,0:T(8,128)} async-done(((f32[8192,256]{1,0:T(8,128)}), f32[2048,256]{1,0:T(8,128)}) %reduce-scatter.19.cloned.1.call-update) | async-done | bytes 2097168 | tf_op jit(solution)/shard_map/reduce_scatter | solution.py:39
  2576.9 18.7 all-reduce.2
  2595.6 52.6 %reduce-scatter.15.cloned.1.call-done = f32[2048,256]{1,0:T(8,128)} async-done(((f32[8192,256]{1,0:T(8,128)}), f32[2048,256]{1,0:T(8,128)}) %reduce-scatter.15.cloned.1.call-update) | async-done | bytes 2097168 | tf_op jit(solution)/shard_map/reduce_scatter | solution.py:39
  2656.3 34.4 %all-gather.21.cloned.1.call-done = bf16[8192,256]{1,0:T(8,128)(2,1)} async-done(((bf16[2048,256]{1,0:T(8,128)(2,1)}), bf16[8192,256]{1,0:T(8,128)(2,1)}) %all-gather.21.cloned.1.call-update) | async-done | bytes 4194320 | tf_op jit(solution)/shard_map/all_gather | solution.py:34
  2697.5 144.5 %reduce-scatter.21.cloned.1.call-done = f32[2048,256]{1,0:T(8,128)} async-done(((f32[8192,256]{1,0:T(8,128)}), f32[2048,256]{1,0:T(8,128)}) %reduce-scatter.21.cloned.1.call-update) | async-done | bytes 2097168 | tf_op jit(solution)/shard_map/reduce_scatter | solution.py:179
  2850.5 82.9 %while.60 = (s32[]{:T(128)}, bf16[2,1024,4,64]{1,3,2,0:T(8,128)(2,1)}, bf16[2,1024,4,64]{1,3,2,0:T(8,128)(2,1)}, bf16[2,1024,4,64]{1,3,2,0:T(8,128)(2,1)}, bf16[...) while((s32[]{:T(128)}, ...), condition=%wide.region_29.30_spmd.clone, body=%wide.region_25.29_spmd.clone.sunk | while | flops 1369307648 | bytes 93416672 | solution.py:226
  2856.5 29.5 while.62
  2897.8 29.5 while.62
  2941.6 219.0 %all-gather.23.cloned.1.call-done = bf16[8192,768]{0,1:T(8,128)(2,1)} async-done(((bf16[2048,768]{0,1:T(8,128)(2,1)}), bf16[8192,768]{0,1:T(8,128)(2,1)}) %all-gather.23.cloned.1.call-update) | async-done | bytes 12582928 | tf_op jit(solution)/shard_map/all_gather | solution.py:232
  3172.1 14.9 fusion.77
  3244.7 13.8 all-reduce
  3258.5 18.7 all-reduce.1
  3282.0 50.2 %all-reduce.9.cloned.1.call-done = (f32[256,768]{1,0:T(8,128)}, f32[256,256]{1,0:T(8,128)}, f32[256,1024]{1,0:T(8,128)}, f32[1024,256]{1,0:T(8,128)}) async-done(((f32[256,768]{1,0:T(8,128)}, f32[256,256]{1,0:T(8,128)}, f32[256,1024]{1,0:T(8,128)}, f32[1024,256]{1,0:T(8,128)}), (f32[256,768]{1,0:T(8,128)}, f32[256,256]{1,0:T(8,128)}, f32[256,1024]{1,0:T(8,128)}, ...) | async-done | bytes 3145744 | tf_op jit(solution)/shard_map/psum | solution.py:241
  (295 shorter events, 307.5 us)
Async XLA Ops:
  7.2 797.1 %copy-start = (bf16[256,1024]{1,0:T(8,128)(2,1)S(1)}, bf16[256,1024]{1,0:T(8,128)(2,1)}, u32[]{:S(2)}) copy-start(bf16[256,1024]{1,0:T(8,128)(2,1)} %param.31) | copy-start | bytes 1572868
  7.2 58.5 %copy-start.11 = (bf16[256,768]{1,0:T(8,128)(2,1)S(1)}, bf16[256,768]{1,0:T(8,128)(2,1)}, u32[]{:S(2)}) copy-start(bf16[256,768]{1,0:T(8,128)(2,1)} %param.25) | copy-start | bytes 1179652
  7.2 58.5 %all-gather.9.cloned.1.call-start = ((), (), s32[]{:S(2)}) async-start(), calls=%async_computation.8 | async-start | bytes 5242880 | tf_op jit(solution)/shard_map/all_gather | solution.py:34
  32.9 461.4 %reduce-scatter.9.cloned.1.call-start = ((), (), s32[]{:S(2)}) async-start(), calls=%async_computation.9 | async-start | bytes 31457280 | tf_op jit(solution)/shard_map/reduce_scatter | solution.py:120
  79.7 575.0 %all-gather.11.cloned.1.call-start = ((), (), s32[]{:S(2)}) async-start(), calls=%async_computation.10 | async-start | bytes 5242880 | tf_op jit(solution)/shard_map/all_gather | solution.py:154
  517.4 137.3 %copy-start.15 = (bf16[256,256]{1,0:T(8,128)(2,1)S(1)}, bf16[256,256]{1,0:T(8,128)(2,1)}, u32[]{:S(2)}) copy-start(bf16[256,256]{1,0:T(8,128)(2,1)} %param.27) | copy-start | bytes 393220
  572.0 159.9 %reduce-scatter.11.cloned.1.call-start = ((), (), s32[]{:S(2)}) async-start(), calls=%async_computation.11 | async-start | bytes 10485760 | tf_op jit(solution)/shard_map/reduce_scatter | solution.py:39
  661.5 70.4 %copy-start.30 = (f32[256]{0:T(256)S(1)}, f32[256]{0:T(256)}, u32[]{:S(2)}) copy-start(f32[256]{0:T(256)} %param.28) | copy-start | bytes 3076
  661.5 91.6 %copy-start.20 = (f32[256]{0:T(256)S(1)}, f32[256]{0:T(256)}, u32[]{:S(2)}) copy-start(f32[256]{0:T(256)} %param.29) | copy-start | bytes 3076
  661.5 91.6 %copy-start.28 = (f32[256]{0:T(256)S(1)}, f32[256]{0:T(256)}, u32[]{:S(2)}) copy-start(f32[256]{0:T(256)} %param.30) | copy-start | bytes 3076
  661.5 106.3 %all-gather.17.cloned.1.call-start = ((), (), s32[]{:S(2)}) async-start(), calls=%async_computation.16 | async-start | bytes 5242880 | tf_op jit(solution)/shard_map/all_gather | solution.py:34
  662.1 105.7 %copy-start.14 = (bf16[1024,256]{1,0:T(8,128)(2,1)S(1)}, bf16[1024,256]{1,0:T(8,128)(2,1)}, u32[]{:S(2)}) copy-start(bf16[1024,256]{1,0:T(8,128)(2,1)} %param.33) | copy-start | bytes 1572868
  662.1 142.2 %all-gather.13.cloned.1.call-start = ((), (), s32[]{:S(2)}) async-start(), calls=%async_computation.12 | async-start | bytes 5242880 | tf_op jit(solution)/shard_map/all_gather | solution.py:34
  754.6 604.1 %reduce-scatter.17.cloned.1.call-start = ((), (), s32[]{:S(2)}) async-start(), calls=%async_computation.17 | async-start | bytes 41943040 | tf_op jit(solution)/shard_map/reduce_scatter | solution.py:51
  784.4 1129.6 %reduce-scatter.13.cloned.1.call-start = ((), (), s32[]{:S(2)}) async-start(), calls=%async_computation.13 | async-start | bytes 41943040 | tf_op jit(solution)/shard_map/reduce_scatter | solution.py:51
  820.2 1093.8 %copy-start.26 = (f32[1024]{0:T(1024)S(1)}, f32[1024]{0:T(1024)}, u32[]{:S(2)}) copy-start(f32[1024]{0:T(1024)} %param.32) | copy-start | bytes 12292
  820.2 1394.6 %all-gather.19.cloned.1.call-start = ((), (), s32[]{:S(2)}) async-start(), calls=%async_computation.18 | async-start | bytes 20971520 | tf_op jit(solution)/shard_map/all_gather | solution.py:62
  1927.2 574.1 %all-gather.15.cloned.1.call-start = ((), (), s32[]{:S(2)}) async-start(), calls=%async_computation.14 | async-start | bytes 20971520 | tf_op jit(solution)/shard_map/all_gather | solution.py:62
  1927.8 646.0 %reduce-scatter.19.cloned.1.call-start = ((), (), s32[]{:S(2)}) async-start(), calls=%async_computation.19 | async-start | bytes 10485760 | tf_op jit(solution)/shard_map/reduce_scatter | solution.py:39
  2229.1 419.1 %reduce-scatter.15.cloned.1.call-start = ((), (), s32[]{:S(2)}) async-start(), calls=%async_computation.15 | async-start | bytes 10485760 | tf_op jit(solution)/shard_map/reduce_scatter | solution.py:39
  2516.4 131.8 %copy-start.29 = (f32[256]{0:T(256)S(1)}, f32[256]{0:T(256)}, u32[]{:S(2)}) copy-start(f32[256]{0:T(256)} %param.34) | copy-start | bytes 3076
  2516.4 174.3 %all-gather.21.cloned.1.call-start = ((), (), s32[]{:S(2)}) async-start(), calls=%async_computation.20 | async-start | bytes 5242880 | tf_op jit(solution)/shard_map/all_gather | solution.py:34
  2656.1 186.0 %reduce-scatter.21.cloned.1.call-start = ((), (), s32[]{:S(2)}) async-start(), calls=%async_computation.21 | async-start | bytes 10485760 | tf_op jit(solution)/shard_map/reduce_scatter | solution.py:179
  2697.4 463.2 %all-gather.23.cloned.1.call-start = ((), (), s32[]{:S(2)}) async-start(), calls=%async_computation.22 | async-start | bytes 15728640 | tf_op jit(solution)/shard_map/all_gather | solution.py:232
  2938.8 221.8 %copy-start.12 = (bf16[256,768]{1,0:T(8,128)(2,1)S(1)}, bf16[256,768]{1,0:T(8,128)(2,1)}, u32[]{:S(2)}) copy-start(bf16[256,768]{1,0:T(8,128)(2,1)} %param.25) | copy-start | bytes 1179652
  2941.5 300.6 %reduce-scatter.23.cloned.1.call-start = ((), (), s32[]{:S(2)}) async-start(), calls=%async_computation.23 | async-start | bytes 10485760 | tf_op jit(solution)/shard_map/reduce_scatter | solution.py:39
  3172.0 160.2 %all-reduce.9.cloned.1.call-start = ((), (), s32[]{:S(2)}) async-start(), calls=%async_computation.24 | async-start | bytes 6291456 | tf_op jit(solution)/shard_map/psum | solution.py:241
  3216.5 28.2 copy-start.22
  3216.5 28.2 copy-start.23
  3216.5 28.2 copy-start.24
  3216.5 28.2 copy-start.25
  3277.3 62.1 %copy-start.1 = (bf16[256,1024]{1,0:T(8,128)(2,1)S(1)}, bf16[256,1024]{1,0:T(8,128)(2,1)}, u32[]{:S(2)}) copy-start(bf16[256,1024]{1,0:T(8,128)(2,1)} %param.31) | copy-start | bytes 1572868
  (25 other events, 160.4 us)
Sparse Core Ops, SparseCore 0:
  33.0 32.6 all-gather.8
  79.8 414.4 reduce-scatter.8
  572.1 82.5 all-gather.10
  661.6 70.2 reduce-scatter.10
  733.3 34.4 all-gather.16
  769.8 34.4 all-gather.12
  806.6 552.0 reduce-scatter.16
  1361.2 552.7 reduce-scatter.12
  1927.3 287.4 all-gather.18
  2216.3 284.9 all-gather.14
  2503.9 69.8 reduce-scatter.18
  2576.4 71.6 reduce-scatter.14
  2656.2 34.4 all-gather.20
  2697.6 144.4 reduce-scatter.20
  2941.7 218.9 all-gather.22
  3172.1 69.8 reduce-scatter.22
  3245.7 86.4 all-reduce.8
where the time goes:
time: 3350 us
  waiting for transfers between devices  2860 us (85%)
  matrix products  197 us (6%)
  blocking collectives  96 us (3%)
  other arithmetic  86.7 us (3%)
  local copies, waits for them, and re-layouts  79.2 us (2%)
    reduce_scatter x2, waiting for transfers between devices, hidden_share(): lax.psum_scatter(lax.dot_general(whole, weight, (((1,), (axis_right,)), (...  1090 us
    all_gather x2, waiting for transfers between devices, hidden_rows(): return lax.all_gather(value, 'row', axis=0, tiled=True)  559 us
    reduce_scatter x1, waiting for transfers between devices, on_device(): lax.psum_scatter(jnp.dot(piece, w_qkv, preferred_element_type=jnp.float32...  414 us
    all_gather x1, waiting for transfers between devices, on_device(): lax.all_gather(grad_joined.astype(jnp.bfloat16), 'row', axis=0, tiled=True)  219 us
    reduce_scatter x4, waiting for transfers between devices, sum_cols(): lax.psum_scatter(lax.dot_general(whole, weight, (((1,), (axis_right,)), (...  193 us
    reduce_scatter x1, waiting for transfers between devices, on_device(): lax.psum_scatter(lax.dot_general(piece, w_out, (((1,), (1,)), ((), ())),...  145 us
    all_gather x4, waiting for transfers between devices, gather_cols(): return lax.all_gather(value, 'col', axis=0, tiled=True)  100 us
    all_gather x1, waiting for transfers between devices, on_device(): context_all = lax.all_gather(context, 'row', axis=0, tiled=True)  82.7 us
  transfers between devices with their start and end apart: 17, of which 17 were waited for; matrix products, arithmetic and copies ran while one was open for 4% of the time, Pallas kernels for 0%

commit v1 on v0

v1 whole, which is shorter than its diff:
```python
import functools

import jax
import jax.numpy as jnp
from jax import lax
from jax.experimental import pallas as pl
from jax.experimental.pallas import tpu as pltpu
from jax.sharding import Mesh, PartitionSpec as P

D = 1024
HEADS = 16
HEAD = 64
LEN = 1024
EPSILON = 1e-05
BLOCK = 256
LOW = jnp.bfloat16
F32 = jnp.float32
SWAP = [(0, 1), (1, 0)]


def dot(left, right, left_axis, right_axis):
    return lax.dot_general(
        left, right, (((left_axis,), (right_axis,)), ((), ())), preferred_element_type=F32
    )


def swap(value):
    return lax.ppermute(value, "core", SWAP)


def half_of(value, which):
    rows = value.shape[0] // 2
    return lax.dynamic_slice_in_dim(value, which * rows, rows, 0)


def join_cores(value):
    first = lax.axis_index("core") == 0
    other = swap(value)
    return jnp.concatenate(
        [jnp.where(first, value, other), jnp.where(first, other, value)], 0
    )


def sum_cores(partial):
    core = lax.axis_index("core")
    return half_of(partial, core) + swap(half_of(partial, 1 - core))


def tokens_in(value):
    rows, width = value.shape
    core = lax.axis_index("core")
    halves = value.reshape(rows // LEN, 2, LEN // 2, width)
    mine = lax.dynamic_index_in_dim(halves, core, 1, False)
    other = swap(lax.dynamic_index_in_dim(halves, 1 - core, 1, False))
    both = jnp.concatenate(
        [jnp.where(core == 0, mine, other), jnp.where(core == 0, other, mine)], 0
    ).reshape(rows, width)
    return lax.all_to_all(both, "row", 0, 1, tiled=True)


def tokens_out(value):
    core = lax.axis_index("core")
    both = lax.all_to_all(value, "row", 1, 0, tiled=True)
    rows, width = both.shape
    parts = both.reshape(2, rows // LEN, LEN // 2, width)
    mine = lax.dynamic_index_in_dim(parts, core, 0, False)
    other = swap(lax.dynamic_index_in_dim(parts, 1 - core, 0, False))
    return jnp.stack(
        [jnp.where(core == 0, mine, other), jnp.where(core == 0, other, mine)], 1
    ).reshape(rows, width)


def ring(axis, step):
    count = lax.axis_size(axis)
    return [(i, (i + step) % count) for i in range(count)]


def gather_axis(value, axis):
    count, me = lax.axis_size(axis), lax.axis_index(axis)
    held = [value] + [lax.ppermute(value, axis, ring(axis, -k)) for k in range(1, count)]
    if count == 2:
        return jnp.where(me == 0, jnp.stack(held), jnp.stack(held[::-1]))
    return jnp.take(jnp.stack(held), (jnp.arange(count) - me) % count, axis=0)


def scatter_axis(value, axis):
    count, me = lax.axis_size(axis), lax.axis_index(axis)
    total = lax.dynamic_index_in_dim(value, me, 0, False).astype(F32)
    for k in range(1, count):
        block = lax.dynamic_index_in_dim(value, (me + k) % count, 0, False)
        total = total + lax.ppermute(block.astype(LOW), axis, ring(axis, k)).astype(F32)
    return total


def gather_weight(weight, row_first):
    rows, width = weight.shape
    size = lax.axis_size("dp")
    me = lax.axis_index("dp")
    piece = rows // 2 // size
    wanted = (["row", "y"] if row_first else ["y", "row"]) + ["dp", "rows", "width"]
    halves = []
    for half, axes in enumerate((("row", "y", "dp"), ("row", "dp", "y"))):
        part = lax.dynamic_slice_in_dim(weight, half * (rows // 2) + me * piece, piece, 0)
        for axis in axes:
            part = gather_axis(part, axis)
        names = list(axes[::-1]) + ["rows", "width"]
        part = part.transpose([names.index(name) for name in wanted])
        halves.append(part.reshape(part.shape[:2] + (rows // 2, width)))
    return jnp.concatenate(halves, 2)


def scatter_grad(grad, row_first):
    rows, width = grad.shape[2:]
    count = lax.axis_size("dp")
    names = (["row", "y"] if row_first else ["y", "row"]) + ["half", "dp", "rows", "width"]
    grad = grad.reshape(grad.shape[:2] + (2, count, rows // 2 // count, width))
    halves = []
    for half, axes in enumerate((("dp", "y", "row"), ("y", "dp", "row"))):
        order = ["half"] + list(axes) + ["rows", "width"]
        part = grad.transpose([names.index(name) for name in order])[half]
        for axis in axes:
            part = scatter_axis(part, axis)
        part = gather_axis(part.astype(LOW), "dp")
        halves.append(part.reshape(rows // 2, width))
    return jnp.concatenate(halves, 0).astype(F32)


def norm_forward(values, gain, shift):
    center = jnp.sum(values, 1, keepdims=True) / D
    spread = jnp.sum(values * values, 1, keepdims=True) / D - center * center
    inverse = lax.rsqrt(spread + EPSILON)
    scaled = (values - center) * inverse
    return (scaled * gain + shift).astype(LOW), scaled, inverse


def norm_backward(grad_normed, scaled, inverse, gain):
    product = grad_normed * gain
    first = jnp.sum(product, 1, keepdims=True) / D
    second = jnp.sum(product * scaled, 1, keepdims=True) / D
    grad_values = inverse * (product - first - scaled * second)
    return grad_values, jnp.sum(grad_normed * scaled, 0), jnp.sum(grad_normed, 0)


def scores_block(keys, query, slope, index):
    count = keys.shape[0]
    raw = dot(keys, query, 1, 1)
    key_place = lax.broadcasted_iota(jnp.int32, (count, 1), 0)
    query_place = lax.broadcasted_iota(jnp.int32, (1, BLOCK), 1) + index * BLOCK
    distance = query_place.astype(F32) - key_place.astype(F32)
    scores = raw - slope * distance
    edge = count - BLOCK
    seen = key_place[edge:] <= query_place
    last = jnp.where(seen, scores[edge:], -jnp.inf)
    return last if edge == 0 else jnp.concatenate([scores[:edge], last], 0)


def attend_kernel(slope_ref, joined_ref, context_ref, log_ref):
    step = pl.program_id(0)
    for index in range(LEN // BLOCK):
        end = (index + 1) * BLOCK
        rows = pl.ds(index * BLOCK, BLOCK)
        parts = []
        for head in range(2):
            base = head * 3 * HEAD
            query = joined_ref[0, rows, base : base + HEAD] * LOW(0.125)
            keys = joined_ref[0, :end, base + HEAD : base + 2 * HEAD]
            values = joined_ref[0, :end, base + 2 * HEAD : base + 3 * HEAD]
            scores = scores_block(keys, query, slope_ref[step * 2 + head], index)
            top = jnp.max(scores, 0, keepdims=True)
            expo = jnp.exp(scores - top)
            total = jnp.sum(expo, 0, keepdims=True)
            parts.append(dot(values, expo.astype(LOW), 0, 0) * (1.0 / total))
            log_ref[0, head : head + 1, rows] = top + jnp.log(total)
        context_ref[0, rows, :] = jnp.concatenate(parts, 0).T.astype(LOW)


def attend_back_kernel(slope_ref, joined_ref, grad_ref, log_ref, out_ref, keys_acc, values_acc):
    step = pl.program_id(0)
    for index in reversed(range(LEN // BLOCK)):
        end = (index + 1) * BLOCK
        rows = pl.ds(index * BLOCK, BLOCK)
        for head in range(2):
            base = head * 3 * HEAD
            query = joined_ref[0, rows, base : base + HEAD] * LOW(0.125)
            keys = joined_ref[0, :end, base + HEAD : base + 2 * HEAD]
            values = joined_ref[0, :end, base + 2 * HEAD : base + 3 * HEAD]
            grad = grad_ref[0, rows, head * HEAD : (head + 1) * HEAD]
            scores = scores_block(keys, query, slope_ref[step * 2 + head], index)
            probs = jnp.exp(scores - log_ref[0, head : head + 1, rows])
            grad_probs = dot(values, grad, 1, 1)
            weighted = probs * grad_probs
            inner = jnp.sum(weighted, 0, keepdims=True)
            grad_scores = (weighted - probs * inner).astype(LOW)
            grad_query = dot(keys, grad_scores, 0, 0) * 0.125
            out_ref[0, rows, base : base + HEAD] = grad_query.T.astype(LOW)
            grad_keys = dot(grad_scores, query, 1, 0)
            grad_values = dot(probs.astype(LOW), grad, 1, 0)
            if end == LEN:
                keys_acc[head] = grad_keys
                values_acc[head] = grad_values
            else:
                keys_acc[head, :end] += grad_keys
                values_acc[head, :end] += grad_values
    for head in range(2):
        base = head * 3 * HEAD
        out_ref[0, :, base + HEAD : base + 2 * HEAD] = keys_acc[head].astype(LOW)
        out_ref[0, :, base + 2 * HEAD : base + 3 * HEAD] = values_acc[head].astype(LOW)


VMEM_LIMIT = 48 * 1024 * 1024


def pair_spec(width, pairs, count):
    return pl.BlockSpec(
        (1, LEN, width),
        lambda step, seq: (step // pairs, seq, step % pairs),
    )


def attend(joined, slopes):
    blocks, tokens, width = joined.shape
    pairs = width // (6 * HEAD)
    count = tokens // LEN
    return pl.pallas_call(
        attend_kernel,
        grid=(blocks * pairs, count),
        in_specs=[
            pl.BlockSpec(memory_space=pltpu.SMEM),
            pair_spec(6 * HEAD, pairs, count),
        ],
        out_specs=[
            pair_spec(2 * HEAD, pairs, count),
            pl.BlockSpec((1, 2, LEN), lambda step, seq: (step, 0, seq)),
        ],
        out_shape=[
            jax.ShapeDtypeStruct((blocks, tokens, width // 3), LOW),
            jax.ShapeDtypeStruct((blocks * pairs, 2, tokens), F32),
        ],
        compiler_params=pltpu.CompilerParams(vmem_limit_bytes=VMEM_LIMIT),
        cost_estimate=pl.CostEstimate(
            flops=40_000_000_000, bytes_accessed=8_000_000, transcendentals=0
        ),
        name="attend",
    )(slopes, joined)


def attend_back(joined, grad_context, logs, slopes):
    blocks, tokens, width = joined.shape
    pairs = width // (6 * HEAD)
    count = tokens // LEN
    return pl.pallas_call(
        attend_back_kernel,
        grid=(blocks * pairs, count),
        in_specs=[
            pl.BlockSpec(memory_space=pltpu.SMEM),
            pair_spec(6 * HEAD, pairs, count),
            pair_spec(2 * HEAD, pairs, count),
            pl.BlockSpec((1, 2, LEN), lambda step, seq: (step, 0, seq)),
        ],
        out_specs=pair_spec(6 * HEAD, pairs, count),
        out_shape=jax.ShapeDtypeStruct(joined.shape, LOW),
        scratch_shapes=[pltpu.VMEM((2, LEN, HEAD), F32), pltpu.VMEM((2, LEN, HEAD), F32)],
        compiler_params=pltpu.CompilerParams(vmem_limit_bytes=VMEM_LIMIT),
        cost_estimate=pl.CostEstimate(
            flops=80_000_000_000, bytes_accessed=12_000_000, transcendentals=0
        ),
        name="attend_back",
    )(slopes, joined, grad_context, logs)


def on_device(
    x_in,
    ln1_gain,
    ln1_bias,
    w_qkv,
    bias_qv,
    w_out,
    b_out,
    ln2_gain,
    ln2_bias,
    w_up,
    b_up,
    w_down,
    b_down,
    grad_out,
):
    row = lax.axis_index("row")
    column = lax.axis_index("y")
    core = lax.axis_index("core")
    row_count = lax.axis_size("row")
    blocks = lax.axis_size("y")
    part = x_in.shape[1]
    local_heads = w_qkv.shape[1] // (3 * HEAD)
    hidden_width = w_up.shape[1]
    out_rows = w_out.shape[0]

    block_ids = jnp.arange(blocks) * 2 + core
    head_ids = (block_ids[:, None] * local_heads + jnp.arange(local_heads)).reshape(-1)
    slopes = 2.0 ** (-8.0 * (head_ids.astype(F32) + 1.0) / HEADS)

    inputs = tokens_in(x_in).astype(F32)
    small = jnp.concatenate(
        [ln1_gain, ln1_bias, b_out, ln2_gain, ln2_bias, b_down, bias_qv, b_up]
    )
    small_all = lax.all_gather(small, ("row", "y"), axis=0).reshape(row_count, blocks, -1)
    by_feature = small_all[:, 0, : 6 * part].reshape(row_count, 6, part)
    by_feature = by_feature.transpose(1, 0, 2).reshape(6, D)
    gain_one, shift_one, bias_out, gain_two, shift_two, bias_down = by_feature
    pair = small_all[0, :, 6 * part : 6 * part + bias_qv.shape[0]]
    pair = pair.reshape(blocks, local_heads, 2, HEAD)
    full_bias = jnp.stack(
        [pair[:, :, 0], jnp.zeros_like(pair[:, :, 0]), pair[:, :, 1]], 2
    ).reshape(blocks, 1, -1)
    bias_up = small_all[0, :, 6 * part + bias_qv.shape[0] :].reshape(blocks, 1, -1)

    qkv_all = gather_weight(w_qkv, False).reshape(blocks, D, -1)
    out_all = gather_weight(w_out, True)
    out_all = out_all.transpose(1, 2, 0, 3).reshape(blocks, out_rows, D)
    up_all = gather_weight(w_up, False).reshape(blocks, D, -1)
    down_all = gather_weight(w_down, True)
    down_all = down_all.transpose(1, 2, 0, 3).reshape(blocks, hidden_width, D)

    normed_one, scaled_one, inverse_one = norm_forward(inputs, gain_one, shift_one)
    normed_one = join_cores(normed_one)
    joined = jnp.stack(
        [
            (dot(normed_one, qkv_all[i], 1, 0) + full_bias[i]).astype(LOW)
            for i in range(blocks)
        ]
    )
    context, logs = attend(joined, slopes)
    mixed = sum(dot(context[i], out_all[i], 1, 0) for i in range(blocks))
    middle = inputs + sum_cores(mixed) + bias_out
    normed_two, scaled_two, inverse_two = norm_forward(middle, gain_two, shift_two)
    normed_two = join_cores(normed_two)
    active, slope_of = [], []
    for i in range(blocks):
        hidden = dot(normed_two, up_all[i], 1, 0) + bias_up[i]
        bent = jnp.tanh(0.7978845608028654 * (hidden + 0.044715 * hidden * hidden * hidden))
        active.append((0.5 * hidden * (1.0 + bent)).astype(LOW))
        slope_of.append(
            0.5 * (1.0 + bent)
            + 0.5
            * hidden
            * (1.0 - bent * bent)
            * 0.7978845608028654
            * (1.0 + 3.0 * 0.044715 * hidden * hidden)
        )
    lifted = sum(dot(active[i], down_all[i], 1, 0) for i in range(blocks))
    out = (middle + sum_cores(lifted) + bias_down).astype(LOW)
    out = tokens_out(out)

    grad_low = tokens_in(grad_out)
    cotangent = grad_low.astype(F32)
    grad_b_down = jnp.sum(cotangent, 0)
    grad_all = join_cores(grad_low)

    def split_columns(parts):
        whole = jnp.stack([item.astype(LOW) for item in parts])
        return whole.reshape(blocks, -1, row_count, part).transpose(2, 0, 1, 3)

    def split_rows(parts):
        whole = jnp.stack([item.astype(LOW) for item in parts])
        return whole.reshape(blocks, row_count, part, -1)

    grad_down = scatter_grad(
        split_columns([dot(active[i], grad_all, 0, 0) for i in range(blocks)]), True
    )
    grad_hidden = [
        (dot(grad_all, down_all[i], 1, 1) * slope_of[i]).astype(LOW) for i in range(blocks)
    ]
    grad_b_up = jnp.stack([jnp.sum(item.astype(F32), 0) for item in grad_hidden])
    grad_up = scatter_grad(
        split_rows([dot(normed_two, item, 0, 0) for item in grad_hidden]), False
    )
    grad_normed_two = sum_cores(sum(dot(grad_hidden[i], up_all[i], 1, 1) for i in range(blocks)))
    back_two, grad_ln2_gain, grad_ln2_bias = norm_backward(
        grad_normed_two, scaled_two, inverse_two, gain_two
    )
    grad_middle = cotangent + back_two
    grad_b_out = jnp.sum(grad_middle, 0)
    grad_middle_all = join_cores(grad_middle.astype(LOW))
    grad_w_out = scatter_grad(
        split_columns([dot(context[i], grad_middle_all, 0, 0) for i in range(blocks)]),
        True,
    )
    grad_context = jnp.stack(
        [dot(grad_middle_all, out_all[i], 1, 1).astype(LOW) for i in range(blocks)]
    )
    grad_joined = attend_back(joined, grad_context, logs, slopes)
    totals = jnp.sum(grad_joined.astype(F32), 1).reshape(blocks, local_heads, 3, HEAD)
    grad_bias_qv = jnp.stack([totals[:, :, 0], totals[:, :, 2]], 2).reshape(blocks, -1)
    grad_qkv = scatter_grad(
        split_rows([dot(normed_one, grad_joined[i], 0, 0) for i in range(blocks)]),
        False,
    )
    grad_normed_one = sum_cores(sum(dot(grad_joined[i], qkv_all[i], 1, 1) for i in range(blocks)))
    back_one, grad_ln1_gain, grad_ln1_bias = norm_backward(
        grad_normed_one, scaled_one, inverse_one, gain_one
    )
    grad_input = tokens_out((grad_middle + back_one).astype(LOW))

    features = jnp.stack(
        [grad_ln1_gain, grad_ln1_bias, grad_b_out, grad_ln2_gain, grad_ln2_bias, grad_b_down]
    )
    columns = jnp.concatenate([grad_bias_qv, grad_b_up], 1)
    features = features + swap(features)
    sums = lax.psum(
        jnp.concatenate([features.reshape(-1), columns.reshape(-1)]), ("dp", "row", "y")
    )
    features = sums[: 6 * D].reshape(6, D)
    features = lax.dynamic_slice_in_dim(features, row * part, part, 1)
    columns = sums[6 * D :].reshape(blocks, -1)
    columns = lax.dynamic_index_in_dim(columns, column, 0, False)
    cut = bias_qv.shape[0]
    return (
        out,
        grad_input,
        features[0],
        features[1],
        grad_qkv,
        columns[:cut],
        grad_w_out,
        features[2],
        features[3],
        features[4],
        grad_up,
        columns[cut:],
        grad_down,
        features[5],
    )


def solution(mesh):
    dp, rows, cols = (mesh.shape[name] for name in ("dp", "row", "col"))
    split = Mesh(mesh.devices.reshape(dp, rows, cols // 2, 2), ("dp", "row", "y", "core"))
    col = ("y", "core")
    token = P(("dp",) + col, "row")
    feature = P("row")
    column = P(col)
    wide = P("row", col)
    tall = P(col, "row")
    in_specs = (
        token,
        feature,
        feature,
        wide,
        column,
        tall,
        feature,
        feature,
        feature,
        wide,
        column,
        tall,
        feature,
        token,
    )
    out_specs = (
        token,
        token,
        feature,
        feature,
        wide,
        column,
        tall,
        feature,
        feature,
        feature,
        wide,
        column,
        tall,
        feature,
    )
    return jax.shard_map(
        on_device, mesh=split, in_specs=in_specs, out_specs=out_specs, check_vma=False
    )
```

time: 3350 us -> 728 us (0.22)
  waiting for transfers between devices: 2860 us -> 125 us
  starting transfers between devices: 1.66 us -> 176 us
  matrix products: 197 us -> 61.6 us
  Pallas kernels: 0 us -> 41.9 us
    reduce_scatter x8 -> x0, waiting for transfers between devices: 1840 us -> none  [the longest x2 1090 us: hidden_share(): lax.psum_scatter(lax.dot_general(whole, weight, (((1,), (axis_right,)), (...]
    all_gather x8 -> x0, waiting for transfers between devices: 961 us -> none  [the longest x2 559 us: hidden_rows(): return lax.all_gather(value, 'row', axis=0, tiled=True)]
    ppermute x0 -> x101, starting transfers between devices: none -> 159 us  [the longest x40 80.5 us: scatter_axis(): lax.ppermute(block.astype(LOW), axis, ring(axis, k)).astype(F32)]
    dot_general x40 -> x24, matrix products: 197 us -> 61.6 us  [dot(): lax.dot_general(left, right, (((left_axis,), (right_axis,)), ((), ())), p...]
    ppermute x0 -> x101, waiting for transfers between devices: none -> 123 us  [the longest x40 77.5 us: scatter_axis(): lax.ppermute(block.astype(LOW), axis, ring(axis, k)).astype(F32)]
    psum x1 -> x0, waiting for transfers between devices: 50.2 us -> none  [on_device(): lax.psum((grad_qkv, grad_bias_qv, grad_w_out, grad_up, grad_b_up, grad_do...]
    pallas_call x0 -> x2, Pallas kernels: none -> 41.9 us  [the longest x1 24.4 us: attend_back(): pl.pallas_call(attend_back_kernel, grid=(blocks * pairs, count), in_specs...]
    select_n x0 -> x43, other arithmetic: none -> 37.4 us  [the longest x32 28.2 us: gather_axis(): return jnp.where(me == 0, jnp.stack(held), jnp.stack(held[::-1]))]
  transfers between devices with their start and end apart: 17 -> 105, of which waited for: 17 -> 34; matrix products, arithmetic and copies ran while one was open for 4% -> 30% of each run, Pallas kernels for 0% -> 6%
where the time goes in v1:
time: 728 us; the launch traced here: 718 us
  starting transfers between devices  176 us (24%)
  waiting for transfers between devices  125 us (17%)
  local copies, waits for them, and re-layouts  112 us (15%)
  blocking collectives  103 us (14%)
  other arithmetic  96.3 us (13%)
  matrix products  61.6 us (8%)
  Pallas kernels  41.9 us (6%)
    ppermute x40, starting transfers between devices, scatter_axis(): lax.ppermute(block.astype(LOW), axis, ring(axis, k)).astype(F32)  80.5 us
    ppermute x40, waiting for transfers between devices, scatter_axis(): lax.ppermute(block.astype(LOW), axis, ring(axis, k)).astype(F32)  77.5 us
    ppermute x48, starting transfers between devices, gather_axis(): lax.ppermute(value, axis, ring(axis, -k))  75.8 us
    psum x1, blocking collectives, on_device(): lax.psum(jnp.concatenate([features.reshape(-1), columns.reshape(-1)]), ('...  72.1 us
    dot_general x24, matrix products, dot(): lax.dot_general(left, right, (((left_axis,), (right_axis,)), ((), ())), p...  61.6 us
    ppermute x48, waiting for transfers between devices, gather_axis(): lax.ppermute(value, axis, ring(axis, -k))  45.3 us
    reshape x5, local copies, waits for them, and re-layouts, scatter_grad(): grad = grad.reshape(grad.shape[:2] + (2, count, rows // 2 // count, width))  32.3 us
    all_gather x1, blocking collectives, on_device(): lax.all_gather(small, ('row', 'y'), axis=0).reshape(row_count, blocks, -1)  30.7 us
  transfers between devices with their start and end apart: 105, of which 34 were waited for; matrix products, arithmetic and copies ran while one was open for 30% of the time, Pallas kernels for 6%

profile of v1, /device:TPU:0, one launch (start us, length us, event | category | flops | bytes accessed | tf_op | source)
XLA Modules:
  0.0 718.4 jit_solution(10465222351146464269)
XLA Ops:
  15.0 30.7 %all-gather = f32[24576]{0:T(1024)S(1)} all-gather(f32[3072]{0:T(1024)S(1)} %constant_dynamic-update-slice_fusion), channel_id=2, replica_groups=mesh['dp'=2,'row'=4,'y'=2,'core'=2] {'row','y'}, dimensions={0}, use_global_device_ids=true | all-gather | bytes 110592 | tf_op jit(solution)/shard_map/all_gather | solution.py:305
  74.2 6.1 collective-permute-start.30
  107.0 4.8 collective-permute-start.40
  131.6 6.9 collective-permute-done.21
  148.6 4.4 all-to-all-start
  177.4 4.4 all-to-all-start.2
  201.3 17.5 %attend.1 = (bf16[2,1024,256]{2,1,0:T(8,128)(2,1)S(1)}, f32[4,2,1024]{2,1,0:T(2,128)S(1)}) custom-call(f32[8]{0:T(128)S(1)} %reshape.900.slope_ref, bf16[2,1024,768]{2,1,0:T(8,128)(2,1)S(1)} %pad_maximum_fusion.1.joined_ref), custom_call_target="tpu_custom_call" | custom-call | flops 40000000000 | bytes 8000000 | tf_op jit(solution)/shard_map/attend/pallas_call | solution.py:224
  235.4 4.0 copy.124
  256.7 4.6 fusion.112
  261.3 5.9 convert_reduce_fusion.2
  276.9 5.7 convert_reduce_fusion.1
  291.8 4.6 convolution_add_fusion.3
  308.7 7.8 %reshape.897 = bf16[4,2,2,2,256,256]{4,3,2,5,0,1:T(2,128)(2,1)} reshape(bf16[4,2,1024,256]{2,3,0,1:T(8,128)(2,1)} %maximum_bitcast_fusion.1) | data formatting | bytes 8388608 | tf_op jit(solution)/shard_map/reshape | solution.py:116
  316.5 11.1 %copy.134 = bf16[4,2,2,2,256,256]{5,4,0,1,3,2:T(8,128)(2,1)} copy(bf16[4,2,2,2,256,256]{4,3,2,5,0,1:T(2,128)(2,1)} %reshape.897) | data formatting | bytes 8388608 | tf_op jit(solution)/shard_map/reshape | solution.py:116
  327.5 11.1 %copy.135 = bf16[4,2,2,2,256,256]{5,4,0,3,1,2:T(8,128)(2,1)} copy(bf16[4,2,2,2,256,256]{4,3,2,5,0,1:T(2,128)(2,1)} %reshape.897) | data formatting | bytes 8388608 | tf_op jit(solution)/shard_map/reshape | solution.py:116
  348.7 16.9 %collective-permute-done.95 = bf16[2,4,256,256]{3,2,1,0:T(8,128)(2,1)S(1)} collective-permute-done((bf16[2,4,256,256]{3,2,1,0:T(8,128)(2,1)S(1)}, bf16[2,4,256,256]{3,2,1,0:T(8,128)(2,1)S(1)}, u32[]{:S(2)}, u32[]{:S(2)}) %collective-permute-start.95) | collective-permute-done | bytes 1048608 | tf_op jit(solution)/shard_map/ppermute | solution.py:91
  371.4 9.2 %collective-permute-done.84 = bf16[4,64,1024]{2,1,0:T(8,128)(2,1)S(1)} collective-permute-done((bf16[4,64,1024]{2,1,0:T(8,128)(2,1)S(1)}, bf16[4,64,1024]{2,1,0:T(8,128)(2,1)S(1)}, u32[]{:S(2)}, u32[]{:S(2)}) %collective-permute-start.84) | collective-permute-done | bytes 524320 | tf_op jit(solution)/shard_map/ppermute | solution.py:91
  384.5 6.3 collective-permute-done.96
  408.2 6.0 collective-permute-done.80
  423.4 4.0 fusion.114
  431.7 4.4 collective-permute-done.92
  438.3 4.1 collective-permute-done.100
  446.5 4.3 all-to-all-start.1
  454.8 24.4 %attend_back.1 = bf16[2,1024,768]{2,1,0:T(8,128)(2,1)S(1)} custom-call(f32[8]{0:T(128)S(1)} %copy-done.4, bf16[2,1024,768]{2,1,0:T(8,128)(2,1)} %copy-done, bf16[2,1024,256]{2,1,0:T(8,128)(2,1)S(1)} %pad_maximum_fusion.18.grad_ref, f32[4,2,1024]{2,1,0:T(2,128)S(1)} %get-tuple-element.21.log_ref), custom_call_target="tpu_custom_call" | custom-call | flops 80000000000 | bytes 12000000 | tf_op jit(solution)/shard_map/attend_back/pallas_call | solution.py:251
  512.0 4.9 collective-permute-start.71
  534.8 8.8 %collective-permute-done.66 = bf16[4,64,256]{2,1,0:T(8,128)(2,1)S(1)} collective-permute-done((bf16[4,64,256]{2,1,0:T(8,128)(2,1)S(1)}, bf16[4,64,256]{2,1,0:T(8,128)(2,1)S(1)}, u32[]{:S(2)}, u32[]{:S(2)}) %collective-permute-start.66) | collective-permute-done | bytes 131104 | tf_op jit(solution)/shard_map/ppermute | solution.py:91
  556.9 13.0 %collective-permute-done.76 = bf16[64,256]{1,0:T(8,128)(2,1)S(1)} collective-permute-done((bf16[64,256]{1,0:T(8,128)(2,1)S(1)}, bf16[64,256]{1,0:T(8,128)(2,1)S(1)}, u32[]{:S(2)}, u32[]{:S(2)}) %collective-permute-start.76) | collective-permute-done | bytes 32800 | tf_op jit(solution)/shard_map/ppermute | solution.py:80
  586.8 4.3 all-to-all-start.3
  596.9 3.9 collective-permute-start.63
  606.0 5.4 collective-permute-done.63
  611.4 17.8 %collective-permute-start.55 = (bf16[64,768]{1,0:T(8,128)(2,1)S(1)}, bf16[64,768]{1,0:T(8,128)(2,1)S(1)}, u32[]{:S(2)}, u32[]{:S(2)}) collective-permute-start(bf16[64,768]{1,0:T(8,128)(2,1)S(1)} %get-tuple-element.90), channel_id=1, source_target_pairs={{0,4},{4,8},{8,12},{12,0},{1,5},{5,9},{9,13},{13,1},{2,6},{6,10},{... | collective-permute-start | bytes 294920 | tf_op jit(solution)/shard_map/ppermute | solution.py:91
  641.5 72.1 %psum.7 = f32[9216]{0:T(1024)S(1)} all-reduce(f32[9216]{0:T(1024)S(1)} %pad_maximum_fusion.35), channel_id=1, replica_groups=mesh['dp'=2,'row'=4,'y'=2,'core'=2] {'dp','row','y'}, use_global_device_ids=true, to_apply=%region_17.22 | all-reduce | flops 9216 | bytes 73728 | tf_op jit(solution)/shard_map/psum | solution.py:408
  (607 shorter events, 376.2 us)
Async XLA Ops:
  1.5 58.6 %collective-permute-start.14 = (bf16[64,256]{1,0:T(8,128)(2,1)S(1)}, bf16[64,256]{1,0:T(8,128)(2,1)S(1)}, u32[]{:S(2)}, u32[]{:S(2)}) collective-permute-start(bf16[64,256]{1,0:T(8,128)(2,1)S(1)} %get-tuple-element.114), channel_id=1, source_target_pairs={{0,4},{4,8},{8,12},{12,0},{1,5},{5,9},{9,13},{13,1},{2,6},{6,10},{... | collective-permute-start | bytes 98312 | tf_op jit(solution)/shard_map/ppermute | solution.py:80
  4.6 56.1 %collective-permute-start.13 = (bf16[64,256]{1,0:T(8,128)(2,1)S(1)}, bf16[64,256]{1,0:T(8,128)(2,1)S(1)}, u32[]{:S(2)}, u32[]{:S(2)}) collective-permute-start(bf16[64,256]{1,0:T(8,128)(2,1)S(1)} %get-tuple-element.114), channel_id=1, source_target_pairs={{0,8},{4,12},{8,0},{12,4},{1,9},{5,13},{9,1},{13,5},{2,10},{6,14},... | collective-permute-start | bytes 98312 | tf_op jit(solution)/shard_map/ppermute | solution.py:80
  7.1 55.0 %collective-permute-start.12 = (bf16[64,256]{1,0:T(8,128)(2,1)S(1)}, bf16[64,256]{1,0:T(8,128)(2,1)S(1)}, u32[]{:S(2)}, u32[]{:S(2)}) collective-permute-start(bf16[64,256]{1,0:T(8,128)(2,1)S(1)} %get-tuple-element.114), channel_id=1, source_target_pairs={{0,12},{4,0},{8,4},{12,8},{1,13},{5,1},{9,5},{13,9},{2,14},{6,2},{... | collective-permute-start | bytes 98312 | tf_op jit(solution)/shard_map/ppermute | solution.py:80
  8.5 54.3 %collective-permute-start.19 = (bf16[64,256]{1,0:T(8,128)(2,1)S(1)}, bf16[64,256]{1,0:T(8,128)(2,1)S(1)}, u32[]{:S(2)}, u32[]{:S(2)}) collective-permute-start(bf16[64,256]{1,0:T(8,128)(2,1)S(1)} %get-tuple-element.115), channel_id=1, source_target_pairs={{0,4},{4,8},{8,12},{12,0},{1,5},{5,9},{9,13},{13,1},{2,6},{6,10},{... | collective-permute-start | bytes 98312 | tf_op jit(solution)/shard_map/ppermute | solution.py:80
  9.2 56.2 %collective-permute-start.18 = (bf16[64,256]{1,0:T(8,128)(2,1)S(1)}, bf16[64,256]{1,0:T(8,128)(2,1)S(1)}, u32[]{:S(2)}, u32[]{:S(2)}) collective-permute-start(bf16[64,256]{1,0:T(8,128)(2,1)S(1)} %get-tuple-element.115), channel_id=1, source_target_pairs={{0,8},{4,12},{8,0},{12,4},{1,9},{5,13},{9,1},{13,5},{2,10},{6,14},... | collective-permute-start | bytes 98312 | tf_op jit(solution)/shard_map/ppermute | solution.py:80
  114.1 30.6 %collective-permute-start = (bf16[2,512,256]{1,2,0:T(8,128)(2,1)}, bf16[2,512,256]{1,2,0:T(8,128)(2,1)}, u32[]{:S(2)}, u32[]{:S(2)}) collective-permute-start(bf16[2,512,256]{1,2,0:T(8,128)(2,1)} %bitcast.2), channel_id=1, source_target_pairs={{0,1},{1,0},{2,3},{3,2},{4,5},{5,4},{6,7},{7,6},{8,9},{9,8},{10,11... | collective-permute-start | bytes 1572872 | tf_op jit(solution)/shard_map/ppermute | solution.py:28
  114.2 49.5 %collective-permute-start.46 = (bf16[2,512,256]{1,2,0:T(8,128)(2,1)}, bf16[2,512,256]{1,2,0:T(8,128)(2,1)}, u32[]{:S(2)}, u32[]{:S(2)}) collective-permute-start(bf16[2,512,256]{1,2,0:T(8,128)(2,1)} %bitcast.132), channel_id=1, source_target_pairs={{0,1},{1,0},{2,3},{3,2},{4,5},{5,4},{6,7},{7,6},{8,9},{9,8},{10,11... | collective-permute-start | bytes 1572872 | tf_op jit(solution)/shard_map/ppermute | solution.py:28
  121.0 32.0 %collective-permute-start.5 = (bf16[4,64,768]{2,1,0:T(8,128)(2,1)}, bf16[4,64,768]{2,1,0:T(8,128)(2,1)}, u32[]{:S(2)}, u32[]{:S(2)}) collective-permute-start(bf16[4,64,768]{2,1,0:T(8,128)(2,1)} %get-tuple-element.144), channel_id=1, source_target_pairs={{0,2},{2,0},{1,3},{3,1},{4,6},{6,4},{5,7},{7,5},{8,10},{10,8},{9,1... | collective-permute-start | bytes 1179656 | tf_op jit(solution)/shard_map/ppermute | solution.py:80
  139.4 27.7 %collective-permute-start.32 = (bf16[4,64,1024]{2,1,0:T(8,128)(2,1)S(1)}, bf16[4,64,1024]{2,1,0:T(8,128)(2,1)}, u32[]{:S(2)}, u32[]{:S(2)}) collective-permute-start(bf16[4,64,1024]{2,1,0:T(8,128)(2,1)S(1)} %get-tuple-element.140), channel_id=1, source_target_pairs={{0,16},{16,0},{1,17},{17,1},{2,18},{18,2},{3,19},{19,3},{4,20},{20... | collective-permute-start | bytes 1572872 | tf_op jit(solution)/shard_map/ppermute | solution.py:80
  148.6 28.7 %all-to-all-start = ((bf16[4,512,256]{1,2,0:T(8,128)(2,1)}), bf16[4,512,256]{1,2,0:T(8,128)(2,1)S(1)}, u32[]{:S(2)}, u32[]{:S(2)}) async-start(bf16[4,512,256]{1,2,0:T(8,128)(2,1)} %pad_maximum_fusion.9), calls=%async_computation | async-start | bytes 2097152 | tf_op jit(solution)/shard_map/all_to_all | solution.py:58
  155.9 26.7 %collective-permute-start.37 = (bf16[4,256,256]{2,1,0:T(8,128)(2,1)S(1)}, bf16[4,256,256]{2,1,0:T(8,128)(2,1)}, u32[]{:S(2)}, u32[]{:S(2)}) collective-permute-start(bf16[4,256,256]{2,1,0:T(8,128)(2,1)S(1)} %get-tuple-element.142), channel_id=1, source_target_pairs={{0,2},{2,0},{1,3},{3,1},{4,6},{6,4},{5,7},{7,5},{8,10},{10,8},{9,1... | collective-permute-start | bytes 1572872 | tf_op jit(solution)/shard_map/ppermute | solution.py:80
  163.6 26.5 %collective-permute-start.6 = (bf16[2,4,64,768]{3,2,1,0:T(8,128)(2,1)}, bf16[2,4,64,768]{3,2,1,0:T(8,128)(2,1)}, u32[]{:S(2)}, u32[]{:S(2)}) collective-permute-start(bf16[2,4,64,768]{3,2,1,0:T(8,128)(2,1)} %maximum_select_fusion.10), channel_id=1, source_target_pairs={{0,16},{16,0},{1,17},{17,1},{2,18},{18,2},{3,19},{19,3},{4,20},{20... | collective-permute-start | bytes 2359304 | tf_op jit(solution)/shard_map/ppermute | solution.py:80
  167.1 26.5 %collective-permute-start.11 = (bf16[2,4,64,768]{3,2,0,1:T(8,128)(2,1)}, bf16[2,4,64,768]{3,2,0,1:T(8,128)(2,1)}, u32[]{:S(2)}, u32[]{:S(2)}) collective-permute-start(bf16[2,4,64,768]{3,2,0,1:T(8,128)(2,1)} %maximum_select_fusion.11), channel_id=1, source_target_pairs={{0,2},{2,0},{1,3},{3,1},{4,6},{6,4},{5,7},{7,5},{8,10},{10,8},{9,1... | collective-permute-start | bytes 2359304 | tf_op jit(solution)/shard_map/ppermute | solution.py:80
  171.2 74.5 %collective-permute-start.33 = (bf16[2,4,64,1024]{3,2,0,1:T(8,128)(2,1)}, bf16[2,4,64,1024]{3,2,0,1:T(8,128)(2,1)}, u32[]{:S(2)}, u32[]{:S(2)}) collective-permute-start(bf16[2,4,64,1024]{3,2,0,1:T(8,128)(2,1)} %maximum_select_fusion.7), channel_id=1, source_target_pairs={{0,2},{2,0},{1,3},{3,1},{4,6},{6,4},{5,7},{7,5},{8,10},{10,8},{9,1... | collective-permute-start | bytes 3145736 | tf_op jit(solution)/shard_map/ppermute | solution.py:80
  173.8 74.1 %collective-permute-start.28 = (bf16[2,4,64,1024]{3,2,1,0:T(8,128)(2,1)}, bf16[2,4,64,1024]{3,2,1,0:T(8,128)(2,1)}, u32[]{:S(2)}, u32[]{:S(2)}) collective-permute-start(bf16[2,4,64,1024]{3,2,1,0:T(8,128)(2,1)} %maximum_select_fusion.6), channel_id=1, source_target_pairs={{0,16},{16,0},{1,17},{17,1},{2,18},{18,2},{3,19},{19,3},{4,20},{20... | collective-permute-start | bytes 3145736 | tf_op jit(solution)/shard_map/ppermute | solution.py:80
  177.4 64.5 %all-to-all-start.2 = ((bf16[4,512,256]{1,2,0:T(8,128)(2,1)}), bf16[4,512,256]{1,2,0:T(8,128)(2,1)}, u32[]{:S(2)}, u32[]{:S(2)}) async-start(bf16[4,512,256]{1,2,0:T(8,128)(2,1)} %pad_maximum_fusion.17), calls=%async_computation.2 | async-start | bytes 2097152 | tf_op jit(solution)/shard_map/all_to_all | solution.py:58
  190.2 40.0 %collective-permute-start.43 = (bf16[2,4,256,256]{3,2,0,1:T(8,128)(2,1)S(1)}, bf16[2,4,256,256]{3,2,0,1:T(8,128)(2,1)S(1)}, u32[]{:S(2)}, u32[]{:S(2)}) collective-permute-start(bf16[2,4,256,256]{3,2,0,1:T(8,128)(2,1)S(1)} %copy-done.56), channel_id=1, source_target_pairs={{0,2},{2,0},{1,3},{3,1},{4,6},{6,4},{5,7},{7,5},{8,10},{10,8},{9,1... | collective-permute-start | bytes 3145736 | tf_op jit(solution)/shard_map/ppermute | solution.py:80
  193.6 39.6 %collective-permute-start.38 = (bf16[2,4,256,256]{3,2,0,1:T(8,128)(2,1)S(1)}, bf16[2,4,256,256]{3,2,0,1:T(8,128)(2,1)S(1)}, u32[]{:S(2)}, u32[]{:S(2)}) collective-permute-start(bf16[2,4,256,256]{3,2,0,1:T(8,128)(2,1)S(1)} %maximum_select_fusion.8), channel_id=1, source_target_pairs={{0,16},{16,0},{1,17},{17,1},{2,18},{18,2},{3,19},{19,3},{4,20},{20... | collective-permute-start | bytes 3145736 | tf_op jit(solution)/shard_map/ppermute | solution.py:80
  290.5 125.6 %collective-permute-start.48 = (f32[512,1024]{0,1:T(8,128)}, f32[512,1024]{0,1:T(8,128)}, u32[]{:S(2)}, u32[]{:S(2)}) collective-permute-start(f32[512,1024]{0,1:T(8,128)} %constant_dynamic-slice_fusion.3), channel_id=1, source_target_pairs={{0,1},{1,0},{2,3},{3,2},{4,5},{5,4},{6,7},{7,6},{8,9},{9,8},{10,11... | collective-permute-start | bytes 6291464 | tf_op jit(solution)/shard_map/ppermute | solution.py:28
  298.7 44.6 %collective-permute-start.83 = (bf16[2,4,64,1024]{3,2,0,1:T(8,128)(2,1)}, bf16[2,4,64,1024]{3,2,0,1:T(8,128)(2,1)}, u32[]{:S(2)}, u32[]{:S(2)}) collective-permute-start(bf16[2,4,64,1024]{3,2,0,1:T(8,128)(2,1)} %dynamic-slice_bitcast_fusion.2), channel_id=1, source_target_pairs={{0,2},{2,0},{1,3},{3,1},{4,6},{6,4},{5,7},{7,5},{8,10},{10,8},{9,1... | collective-permute-start | bytes 3145736 | tf_op jit(solution)/shard_map/ppermute | solution.py:91
  303.5 43.3 %collective-permute-start.77 = (bf16[2,4,64,1024]{3,2,1,0:T(8,128)(2,1)}, bf16[2,4,64,1024]{3,2,1,0:T(8,128)(2,1)S(1)}, u32[]{:S(2)}, u32[]{:S(2)}) collective-permute-start(bf16[2,4,64,1024]{3,2,1,0:T(8,128)(2,1)} %dynamic-slice_bitcast_fusion.3), channel_id=1, source_target_pairs={{0,16},{16,0},{1,17},{17,1},{2,18},{18,2},{3,19},{19,3},{4,20},{20... | collective-permute-start | bytes 3145736 | tf_op jit(solution)/shard_map/ppermute | solution.py:91
  341.7 80.6 %collective-permute-start.44 = (f32[512,1024]{0,1:T(8,128)S(1)}, f32[512,1024]{0,1:T(8,128)S(1)}, u32[]{:S(2)}, u32[]{:S(2)}) collective-permute-start(f32[512,1024]{0,1:T(8,128)S(1)} %constant_dynamic-slice_fusion.6), channel_id=1, source_target_pairs={{0,1},{1,0},{2,3},{3,2},{4,5},{5,4},{6,7},{7,6},{8,9},{9,8},{10,11... | collective-permute-start | bytes 6291464 | tf_op jit(solution)/shard_map/ppermute | solution.py:28
  346.8 33.8 %collective-permute-start.84 = (bf16[4,64,1024]{2,1,0:T(8,128)(2,1)S(1)}, bf16[4,64,1024]{2,1,0:T(8,128)(2,1)S(1)}, u32[]{:S(2)}, u32[]{:S(2)}) collective-permute-start(bf16[4,64,1024]{2,1,0:T(8,128)(2,1)S(1)} %fusion.39), channel_id=1, source_target_pairs={{0,16},{16,0},{1,17},{17,1},{2,18},{18,2},{3,19},{19,3},{4,20},{20... | collective-permute-start | bytes 1572872 | tf_op jit(solution)/shard_map/ppermute | solution.py:91
  446.5 124.5 %all-to-all-start.1 = ((bf16[512,4,256]{0,2,1:T(8,128)(2,1)}), bf16[512,4,256]{0,2,1:T(8,128)(2,1)}, u32[]{:S(2)}, u32[]{:S(2)}) async-start(bf16[512,4,256]{0,2,1:T(8,128)(2,1)} %bitcast.121), calls=%async_computation.1 | async-start | bytes 2097152 | tf_op jit(solution)/shard_map/all_to_all | solution.py:63
  507.1 74.7 %collective-permute-start.50 = (f32[512,1024]{0,1:T(8,128)}, f32[512,1024]{0,1:T(8,128)}, u32[]{:S(2)}, u32[]{:S(2)}) collective-permute-start(f32[512,1024]{0,1:T(8,128)} %constant_dynamic-slice_fusion.2), channel_id=1, source_target_pairs={{0,1},{1,0},{2,3},{3,2},{4,5},{5,4},{6,7},{7,6},{8,9},{9,8},{10,11... | collective-permute-start | bytes 6291464 | tf_op jit(solution)/shard_map/ppermute | solution.py:28
  517.9 54.2 %collective-permute-start.59 = (bf16[2,4,64,768]{3,2,0,1:T(8,128)(2,1)}, bf16[2,4,64,768]{3,2,0,1:T(8,128)(2,1)}, u32[]{:S(2)}, u32[]{:S(2)}) collective-permute-start(bf16[2,4,64,768]{3,2,0,1:T(8,128)(2,1)} %dynamic-slice_bitcast_fusion.4), channel_id=1, source_target_pairs={{0,2},{2,0},{1,3},{3,1},{4,6},{6,4},{5,7},{7,5},{8,10},{10,8},{9,1... | collective-permute-start | bytes 2359304 | tf_op jit(solution)/shard_map/ppermute | solution.py:91
  586.8 52.1 %all-to-all-start.3 = ((bf16[512,4,256]{0,2,1:T(8,128)(2,1)}), bf16[512,4,256]{0,2,1:T(8,128)(2,1)}, u32[]{:S(2)}, u32[]{:S(2)}) async-start(bf16[512,4,256]{0,2,1:T(8,128)(2,1)} %bitcast.140), calls=%async_computation.3 | async-start | bytes 2097152 | tf_op jit(solution)/shard_map/all_to_all | solution.py:63
  600.8 30.0 %collective-permute-start.62 = (bf16[64,768]{1,0:T(8,128)(2,1)S(1)}, bf16[64,768]{1,0:T(8,128)(2,1)S(1)}, u32[]{:S(2)}, u32[]{:S(2)}) collective-permute-start(bf16[64,768]{1,0:T(8,128)(2,1)S(1)} %get-tuple-element.95), channel_id=1, source_target_pairs={{0,8},{4,12},{8,0},{12,4},{1,9},{5,13},{9,1},{13,5},{2,10},{6,14},... | collective-permute-start | bytes 294920 | tf_op jit(solution)/shard_map/ppermute | solution.py:91
  600.8 30.0 %collective-permute-start.61 = (bf16[64,768]{1,0:T(8,128)(2,1)S(1)}, bf16[64,768]{1,0:T(8,128)(2,1)S(1)}, u32[]{:S(2)}, u32[]{:S(2)}) collective-permute-start(bf16[64,768]{1,0:T(8,128)(2,1)S(1)} %get-tuple-element.93), channel_id=1, source_target_pairs={{0,4},{4,8},{8,12},{12,0},{1,5},{5,9},{9,13},{13,1},{2,6},{6,10},{... | collective-permute-start | bytes 294920 | tf_op jit(solution)/shard_map/ppermute | solution.py:91
  602.1 29.3 %collective-permute-start.57 = (bf16[64,768]{1,0:T(8,128)(2,1)S(1)}, bf16[64,768]{1,0:T(8,128)(2,1)S(1)}, u32[]{:S(2)}, u32[]{:S(2)}) collective-permute-start(bf16[64,768]{1,0:T(8,128)(2,1)S(1)} %get-tuple-element.91), channel_id=1, source_target_pairs={{0,12},{4,0},{8,4},{12,8},{1,13},{5,1},{9,5},{13,9},{2,14},{6,2},{... | collective-permute-start | bytes 294920 | tf_op jit(solution)/shard_map/ppermute | solution.py:91
  604.9 29.1 %collective-permute-start.56 = (bf16[64,768]{1,0:T(8,128)(2,1)S(1)}, bf16[64,768]{1,0:T(8,128)(2,1)S(1)}, u32[]{:S(2)}, u32[]{:S(2)}) collective-permute-start(bf16[64,768]{1,0:T(8,128)(2,1)S(1)} %get-tuple-element.92), channel_id=1, source_target_pairs={{0,8},{4,12},{8,0},{12,4},{1,9},{5,13},{9,1},{13,5},{2,10},{6,14},... | collective-permute-start | bytes 294920 | tf_op jit(solution)/shard_map/ppermute | solution.py:91
  640.0 75.6 %collective-permute-start.51 = (bf16[2,512,256]{1,2,0:T(8,128)(2,1)S(1)}, bf16[2,512,256]{1,2,0:T(8,128)(2,1)S(1)}, u32[]{:S(2)}, u32[]{:S(2)}) collective-permute-start(bf16[2,512,256]{1,2,0:T(8,128)(2,1)S(1)} %dynamic-slice_bitcast_fusion.6), channel_id=1, source_target_pairs={{0,1},{1,0},{2,3},{3,2},{4,5},{5,4},{6,7},{7,6},{8,9},{9,8},{10,11... | collective-permute-start | bytes 1572872 | tf_op jit(solution)/shard_map/ppermute | solution.py:28
  (156 other events, 2117.4 us)
